TPU v7x, 256 devices: a whole 4x4x8 slice. The times are simulated.
256 devices in a mesh: blk: 16 (over z_lo, y), grain: 16 (over z_hi, x, core).
Axes of the slice: x: 4, y: 4, z: 8 (z_hi: 2, z_lo: 4; z = z_hi * 4 + z_lo), core: 2. Of those that a mesh axis runs over, the one named last changes fastest.
Arguments:
- order: float32 [256, 512, 2048], P('grain', 'blk'), may hold values from -0.6 to 0.6
- grain_ids: int32 [256], P('grain'), may hold values from 0 to 255, each once
- counts: int32 [16], P('grain'), may hold values from 1 to 16, as said below
- labels: int32 [512, 2048], P('blk'), may hold values from 0 to 255
Outputs:
- evolved: float32 [256, 512, 2048], P('grain', 'blk')
Inputs may be any that keep to these rules, and one draw needn't show every extreme that they name: `counts`: each grain group has 1 to 16 active slots, some group exactly 16.
All inputs are finite; a program needn't handle non-finite values.
Results may differ from a plain program's by a relative error of at most 0.0003.
Values sent between devices are 32-bit elements; how exact they have to be, the bound alone decides.
A program may use at most 128 MiB of HBM per device.

v0:
```python
import jax
import jax.numpy as jnp
from jax import lax
from jax.experimental import pallas as pl
from jax.experimental.pallas import tpu as pltpu
from jax.sharding import PartitionSpec as P

NZ = 32
LANES = 128
SUB = 8
PAIR = 2 * SUB
SLOTS = 16
ROWS = 32
BLKS = 16
HALF = BLKS // 2
CHUNK = 2
NX4 = 4
TILES = ROWS // SUB
STRIDE = BLKS * ROWS
MESH = pl.DeviceIdType.MESH
F32 = jnp.float32
BF16 = jnp.bfloat16

NAMES = (
    ["core_s", "core_pq", "core_e"]
    + [f"x_{a}{d}" for a in ("s", "pq", "e") for d in (1, 2, 3)]
    + [f"z_{a}" for a in ("s", "t")]
    + [f"all_{a}{d}" for a in ("s", "t") for d in (1, 2, 3)]
    + [f"fwd_{a}{d}" for a in ("s", "t") for d in range(4)]
    + [f"halo_{a}{side}" for a in ("eta", "u", "s") for side in (0, 1)]
)
INDEX = {name: i for i, name in enumerate(NAMES)}


def stencil_weights(w):
    k = lax.rem(lax.broadcasted_iota(jnp.int32, (2 * LANES, 2 * LANES), 0), LANES)
    n = lax.broadcasted_iota(jnp.int32, (2 * LANES, 2 * LANES), 1)
    m = lax.rem(n, LANES)
    same_y = lax.div(k, NZ) == lax.div(m, NZ)
    dz = lax.rem(m - k + LANES, NZ)
    z_side = same_y & ((dz == 1) | (dz == NZ - 1))
    y_side = (m - k == NZ) | (k - m == NZ)
    wrap = (m - k == LANES - NZ) | (k - m == LANES - NZ)
    inside = jnp.where(z_side, 1.0, 0.0) + jnp.where(y_side, 1.0, 0.0)
    w[...] = jnp.where(n < LANES, inside, jnp.where(wrap, 1.0, 0.0)).astype(BF16)


def split(c):
    hi = c.astype(BF16)
    lo = (c - hi.astype(F32)).astype(BF16)
    return hi, lo


def kernel(order, ids_hbm, counts, labels, e1, u2, s2, ids, w, x, ya, yb, e0, lab,
           ps, pq, pe, r1s, r1pq, r1e, r2s, r2pq, r2e, part_s, part_t, z_s, z_t, s1,
           h_eta, g_eta, h_u, g_u, h_s, g_s,
           load_sem, lab_sem, small_sem, send_sem, recv_sem):
    b = lax.axis_index("blk")
    g = lax.axis_index("grain")
    nb = lax.axis_size("blk")
    core = lax.rem(g, 2)
    xi = lax.rem(lax.div(g, 2), NX4)
    zh = lax.div(g, 2 * NX4)

    def grain(z, d, c):
        return (b, (z * NX4 + lax.rem(xi + d, NX4)) * 2 + c)

    sibling = grain(zh, 0, 1 - core)
    across = grain(1 - zh, 0, core)
    peer = {d: grain(zh, d, core) for d in (1, 2, 3)}
    after = (lax.rem(b + 1, nb), g)
    before = (lax.rem(b + nb - 1, nb), g)
    toward = (before, after)
    partners = [sibling, across, after, before] + list(peer.values())

    def remote(name, src, dst, who):
        i = INDEX[name]
        return pltpu.make_async_remote_copy(
            src, dst, send_sem.at[i], recv_sem.at[i], device_id=who, device_id_type=MESH)

    def load(j):
        cols = pl.ds(pl.multiple_of(j * LANES, LANES), LANES)
        return pltpu.make_async_copy(order.at[:, :, cols], e0.at[pl.ds(1, SLOTS), j], load_sem.at[j])

    mine = HALF * core
    theirs = HALF * (1 - core)

    def start_load(k, carry):
        load(lax.rem(theirs + k, BLKS)).start()
        return carry

    lax.fori_loop(0, BLKS, start_load, 0)
    ids_copy = pltpu.make_async_copy(ids_hbm, ids, small_sem)
    ids_copy.start()
    lab_copy = pltpu.make_async_copy(labels, lab, lab_sem)
    lab_copy.start()

    barrier = pltpu.get_barrier_semaphore()
    for who in partners:
        pl.semaphore_signal(barrier, inc=1, device_id=who, device_id_type=MESH)

    stencil_weights(w)
    count = counts[0]
    act = [jnp.where(s < count, 1.0, 0.0).astype(F32) for s in range(SLOTS)]

    e0f = e0.reshape((SLOTS + 2) * STRIDE, LANES)
    e1f = e1.reshape((SLOTS + 2) * STRIDE, LANES)
    u2f = u2.reshape(SLOTS * STRIDE, LANES)
    sub = lax.broadcasted_iota(jnp.int32, (SUB, LANES), 0)
    lane = lax.broadcasted_iota(jnp.int32, (SUB, LANES), 1)
    low = lane < LANES // 2
    edge_row = (0, ROWS - 1)

    def at_edge(offset, j, side, half):
        start = (SUB * half + offset) * STRIDE + j * ROWS + edge_row[side]
        return pl.ds(start, SUB, stride=STRIDE)

    def slots_of(half):
        return pl.ds(SUB * half, SUB)

    def chunk(d):
        return pl.ds(mine + CHUNK * lax.rem(xi + NX4 + d, NX4), CHUNK)

    def local(d):
        return CHUNK * lax.rem(xi + NX4 + d, NX4)


    def core_s():
        return remote("core_s", ps.at[pl.ds(theirs, HALF)], r1s, sibling)

    def core_pq():
        return remote("core_pq", pq.at[pl.ds(theirs, HALF)], r1pq, sibling)

    def core_e():
        return remote("core_e", pe.at[pl.ds(theirs, HALF)], r1e, sibling)

    def x_s(d):
        return remote(f"x_s{d}", ps.at[chunk(d)], r2s.at[d - 1], peer[d])

    def x_pq(d):
        return remote(f"x_pq{d}", pq.at[chunk(d)], r2pq.at[d - 1], peer[d])

    def x_e(d):
        return remote(f"x_e{d}", pe.at[chunk(d)], r2e.at[d - 1], peer[d])

    def z_swap(a, part, got):
        return remote(f"z_{a}", part, got, across)

    def gather(a, total, d, got=False):
        where = chunk(-d if got else 0)
        return remote(f"all_{a}{d}", total.at[where], total.at[where], peer[d])

    def forward(a, total, d, got=False):
        where = chunk(-d)
        if got:
            where = pl.ds(theirs + local(-d), CHUNK)
        return remote(f"fwd_{a}{d}", total.at[where], total.at[where], sibling)

    def halo(a, src, dst, side):
        return remote(f"halo_{a}{side}", src.at[side], dst.at[1 - side], toward[side])

    def add_chunk(total, got, d):
        for i in range(CHUNK):
            k = local(d) + i
            total[mine + k] = total[mine + k] + got[k]

    def first_pass(k, carry):
        j = lax.rem(theirs + k, BLKS)
        load(j).wait()
        acc = [jnp.zeros((PAIR, LANES), F32) for _ in range(TILES // 2)]
        for s in range(SLOTS):
            for r in range(TILES // 2):
                rows = pl.ds(PAIR * r, PAIR)
                c = e0[s + 1, j, rows, :] * act[s]
                e0[s + 1, j, rows, :] = c
                acc[r] = acc[r] + c * c
                x[s, j, rows, :LANES], x[s, j, rows, LANES:] = split(c)
        for r in range(TILES // 2):
            ps[j, pl.ds(PAIR * r, PAIR), :] = acc[r]
        for side in range(2):
            for half in range(2):
                h_eta[side, j, slots_of(half), :] = e0f[at_edge(1, j, side, half), :]
        return carry

    def planes(s, y):
        lhs = x[s].reshape(BLKS * ROWS, 2 * LANES)
        y[...] = jnp.dot(lhs, w[...], preferred_element_type=F32)

    def point(src, dst, dst_shift, s, y):
        gid = jnp.where(s < count, ids[s], -1)
        row = (s + 1) * STRIDE
        for j in range(BLKS):
            left = (j + BLKS - 1) % BLKS * ROWS
            right = (j + 1) % BLKS * ROWS
            for r in range(TILES):
                at = row + j * ROWS + SUB * r
                c = src[pl.ds(pl.multiple_of(at, SUB), SUB), :]
                up_x = src[pl.ds(at + 1, SUB), :]
                dn_x = src[pl.ds(at - 1, SUB), :]
                if r == TILES - 1:
                    up_x = jnp.where(sub == SUB - 1, 0.0, up_x)
                if r == 0:
                    dn_x = jnp.where(sub == 0, 0.0, dn_x)
                own = y[j * ROWS + SUB * r:j * ROWS + SUB * r + SUB, :LANES]
                spill = jnp.where(
                    low, y[left + SUB * r:left + SUB * r + SUB, LANES:],
                    y[right + SUB * r:right + SUB * r + SUB, LANES:])
                nb_sum = (up_x + dn_x) + (own + spill)
                labs = lab[pl.ds(SUB * r, SUB), j * LANES:j * LANES + LANES]
                mark = jnp.where(labs == gid, 0.15, 0.0).astype(F32)
                val = 0.15 * nb_sum + c * (0.175 + 0.15 * (c * c)) + mark
                dst[pl.ds(pl.multiple_of(at + dst_shift, SUB), SUB), :] = val

    def linear(src, dst, dst_shift, s_lo, s_hi):
        planes(s_lo, ya)

        def one(i, carry):
            s = s_lo + 2 * i
            planes(s + 1, yb)
            point(src, dst, dst_shift, s, ya)
            planes(jnp.minimum(s + 2, s_hi - 1), ya)
            point(src, dst, dst_shift, s + 1, yb)
            return carry

        lax.fori_loop(0, (s_hi - s_lo) // 2, one, 0)

    def sums_pass(j, carry):
        accp = [jnp.zeros((SUB, LANES), F32) for _ in range(TILES)]
        accq = [jnp.zeros((SUB, LANES), F32) for _ in range(TILES)]
        for s in range(SLOTS):
            for r in range(TILES):
                rows = pl.ds(SUB * r, SUB)
                u = e1[s + 1, j, rows, :]
                accp[r] = accp[r] + u * e0[s + 1, j, rows, :]
                accq[r] = accq[r] + u * u
        for r in range(TILES):
            pq[j, 0, pl.ds(SUB * r, SUB), :] = accp[r]
            pq[j, 1, pl.ds(SUB * r, SUB), :] = accq[r]
        return carry

    def edge_pass(j, carry):
        fix = jnp.zeros((SUB, LANES), F32)
        for side in range(2):
            dp = jnp.zeros((SUB, LANES), F32)
            dq = jnp.zeros((SUB, LANES), F32)
            for half in range(2):
                where = at_edge(1, j, side, half)
                add = 0.15 * g_eta[side, j, slots_of(half), :]
                old = e1f[where, :]
                new = old + add
                e1f[where, :] = new
                h_u[side, j, slots_of(half), :] = new
                dp = dp + add * h_eta[side, j, slots_of(half), :]
                dq = dq + add * (old + new)
            fix = jnp.where(sub == side, jnp.sum(dp, axis=0, keepdims=True), fix)
            fix = jnp.where(sub == side + 2, jnp.sum(dq, axis=0, keepdims=True), fix)
        pe[j] = fix
        return carry

    def second_pass(j, carry):
        tot = [0.225 * s1[j, pl.ds(PAIR * r, PAIR), :] for r in range(TILES // 2)]
        for s in range(SLOTS):
            for r in range(TILES // 2):
                rows = pl.ds(PAIR * r, PAIR)
                v = e1[s + 1, j, rows, :] - e0[s + 1, j, rows, :] * tot[r]
                e1[s + 1, j, rows, :] = v
                x[s, j, rows, :LANES], x[s, j, rows, LANES:] = split(v)
        return carry

    def last_edge_pass(j, carry):
        for side in range(2):
            tot = 0.225 * g_s[side, pl.ds(j, 1), :]
            for half in range(2):
                where = at_edge(0, j, side, half)
                out = g_u[side, j, slots_of(half), :] - g_eta[side, j, slots_of(half), :] * tot
                u2f[where, :] = u2f[where, :] + 0.15 * out
        return carry

    lax.fori_loop(0, HALF, first_pass, 0)
    pl.semaphore_wait(barrier, len(partners))
    core_s().start()
    lax.fori_loop(HALF, BLKS, first_pass, 0)
    for side in range(2):
        halo("eta", h_eta, g_eta, side).start()
    ids_copy.wait()
    lab_copy.wait()
    linear(e0f, e1f, 0, 0, 4)

    core_s().wait_recv()
    for d in (2, 1, 3):
        add_chunk(ps, r1s, d)
        x_s(d).start()
    add_chunk(ps, r1s, 0)
    linear(e0f, e1f, 0, 4, SLOTS)

    lax.fori_loop(theirs, theirs + HALF, sums_pass, 0)
    core_pq().start()
    lax.fori_loop(mine, mine + HALF, sums_pass, 0)

    for d in (1, 3, 2):
        x_s(d).wait_recv()
    for i in range(CHUNK):
        k = mine + local(0) + i
        part_s[i] = (ps[k] + r2s[1, i]) + (r2s[0, i] + r2s[2, i])
    z_swap("s", part_s, z_s).start()

    core_pq().wait_recv()
    for d in (2, 1, 3):
        add_chunk(pq, r1pq, d)
        x_pq(d).start()
    add_chunk(pq, r1pq, 0)

    for side in range(2):
        halo("eta", h_eta, g_eta, side).wait_recv()
    lax.fori_loop(0, HALF, lambda k, c: edge_pass(theirs + k, c), 0, unroll=True)
    core_e().start()
    lax.fori_loop(0, HALF, lambda k, c: edge_pass(mine + k, c), 0, unroll=True)
    for side in range(2):
        halo("u", h_u, g_u, side).start()
    core_e().wait_recv()
    for d in (2, 1, 3):
        add_chunk(pe, r1e, d)
        x_e(d).start()
    add_chunk(pe, r1e, 0)

    z_swap("s", part_s, z_s).wait_recv()
    for i in range(CHUNK):
        s1[mine + local(0) + i] = part_s[i] + z_s[i]
    for d in (2, 1, 3):
        gather("s", s1, d).start()
    forward("s", s1, 0).start()

    for d in (1, 3, 2):
        x_pq(d).wait_recv()
    for d in (1, 3, 2):
        x_e(d).wait_recv()
    for i in range(CHUNK):
        k = mine + local(0) + i
        s = 0.45 * s1[k]
        p_sum = (pq[k, 0] + r2pq[1, i, 0]) + (r2pq[0, i, 0] + r2pq[2, i, 0])
        q_sum = (pq[k, 1] + r2pq[1, i, 1]) + (r2pq[0, i, 1] + r2pq[2, i, 1])
        part_t[i] = q_sum - s * p_sum
        fix = (pe[k] + r2e[1, i]) + (r2e[0, i] + r2e[2, i])
        for side, row in enumerate(edge_row):
            part_t[i, row:row + 1, :] = part_t[i, row:row + 1, :] + (
                fix[side + 2:side + 3] - 0.45 * s1[k, row:row + 1, :] * fix[side:side + 1])
    z_swap("t", part_t, z_t).start()

    for d in (1, 3, 2):
        gather("s", s1, d, True).wait_recv()
        forward("s", s1, d).start()
    lax.fori_loop(mine, mine + HALF, second_pass, 0)

    z_swap("t", part_t, z_t).wait_recv()
    for i in range(CHUNK):
        k = mine + local(0) + i
        s = s1[k]
        s2[k] = (part_t[i] + z_t[i]) + 0.050625 * (s * s * s)
    for d in (2, 1, 3):
        gather("t", s2, d).start()
    forward("t", s2, 0).start()

    for d in range(4):
        forward("s", s1, d, True).wait_recv()
    for side, row in enumerate(edge_row):
        for j in range(BLKS):
            h_s[side, j:j + 1, :] = s1[j, row:row + 1, :]
        halo("s", h_s, g_s, side).start()
    lax.fori_loop(theirs, theirs + HALF, second_pass, 0)
    linear(e1f, u2f, -STRIDE, 0, 12)

    for d in (1, 3, 2):
        gather("t", s2, d, True).wait_recv()
        forward("t", s2, d).start()
    linear(e1f, u2f, -STRIDE, 12, SLOTS)
    for side in range(2):
        halo("u", h_u, g_u, side).wait_recv()
        halo("s", h_s, g_s, side).wait_recv()
    lax.fori_loop(0, BLKS, last_edge_pass, 0, unroll=8)
    for d in range(4):
        forward("t", s2, d, True).wait_recv()

    core_s().wait_send()
    core_pq().wait_send()
    core_e().wait_send()
    for d in (1, 2, 3):
        x_s(d).wait_send()
        x_pq(d).wait_send()
        x_e(d).wait_send()
        gather("s", s1, d).wait_send()
        gather("t", s2, d).wait_send()
    z_swap("s", part_s, z_s).wait_send()
    z_swap("t", part_t, z_t).wait_send()
    for d in range(4):
        forward("s", s1, d).wait_send()
        forward("t", s2, d).wait_send()
    for side in range(2):
        halo("eta", h_eta, g_eta, side).wait_send()
        halo("u", h_u, g_u, side).wait_send()
        halo("s", h_s, g_s, side).wait_send()


def last(e1, u2, s2, out, stage, sem):
    def copy(s):
        return pltpu.make_async_copy(stage.at[s], out.at[s], sem.at[s])

    def one(s, carry):
        def blocks(j, carry):
            cols = pl.ds(pl.multiple_of(j * LANES, LANES), LANES)
            for r in range(TILES):
                rows = pl.ds(SUB * r, SUB)
                stage[s, rows, cols] = u2[s, j, rows, :] - e1[s + 1, j, rows, :] * (0.225 * s2[j, rows, :])
            return carry
        lax.fori_loop(0, BLKS, blocks, 0, unroll=4)
        copy(s).start()
        return carry

    lax.fori_loop(0, SLOTS, one, 0)

    def drain(s, carry):
        copy(s).wait()
        return carry
    lax.fori_loop(0, SLOTS, drain, 0)


def body(order, grain_ids, counts, labels):
    hbm = pl.BlockSpec(memory_space=pltpu.HBM)
    smem = pl.BlockSpec(memory_space=pltpu.SMEM)
    vmem = pl.BlockSpec(memory_space=pltpu.VMEM)
    grain_ids = pltpu.with_memory_space_constraint(grain_ids, pltpu.HBM)
    order = pltpu.with_memory_space_constraint(order, pltpu.HBM)
    labels = pltpu.with_memory_space_constraint(labels, pltpu.HBM)

    def f32(*shape):
        return pltpu.VMEM(shape, F32)

    e1, u2, s2 = pl.pallas_call(
        kernel,
        out_shape=(
            f32(SLOTS + 2, BLKS, ROWS, LANES),
            f32(SLOTS, BLKS, ROWS, LANES),
            f32(BLKS, ROWS, LANES),
        ),
        in_specs=[hbm, hbm, smem, hbm],
        out_specs=(vmem, vmem, vmem),
        scratch_shapes=[
            pltpu.SMEM((SLOTS,), jnp.int32),
            pltpu.VMEM((2 * LANES, 2 * LANES), BF16),
            pltpu.VMEM((SLOTS, BLKS, ROWS, 2 * LANES), BF16),
            f32(BLKS * ROWS, 2 * LANES),
            f32(BLKS * ROWS, 2 * LANES),
            f32(SLOTS + 2, BLKS, ROWS, LANES),
            pltpu.VMEM((ROWS, BLKS * LANES), jnp.int32),
            f32(BLKS, ROWS, LANES),
            f32(BLKS, 2, ROWS, LANES),
            f32(BLKS, SUB, LANES),
            f32(HALF, ROWS, LANES),
            f32(HALF, 2, ROWS, LANES),
            f32(HALF, SUB, LANES),
            f32(3, CHUNK, ROWS, LANES),
            f32(3, CHUNK, 2, ROWS, LANES),
            f32(3, CHUNK, SUB, LANES),
            f32(CHUNK, ROWS, LANES),
            f32(CHUNK, ROWS, LANES),
            f32(CHUNK, ROWS, LANES),
            f32(CHUNK, ROWS, LANES),
            f32(BLKS, ROWS, LANES),
            f32(2, BLKS, SLOTS, LANES),
            f32(2, BLKS, SLOTS, LANES),
            f32(2, BLKS, SLOTS, LANES),
            f32(2, BLKS, SLOTS, LANES),
            f32(2, BLKS, LANES),
            f32(2, BLKS, LANES),
            pltpu.SemaphoreType.DMA((BLKS,)),
            pltpu.SemaphoreType.DMA,
            pltpu.SemaphoreType.DMA,
            pltpu.SemaphoreType.DMA((len(NAMES),)),
            pltpu.SemaphoreType.DMA((len(NAMES),)),
        ],
        compiler_params=pltpu.CompilerParams(
            collective_id=0, has_side_effects=True, vmem_limit_bytes=40 * 1024 * 1024),
        name="steps",
    )(order, grain_ids, counts, labels)
    return pl.pallas_call(
        last,
        out_shape=jax.ShapeDtypeStruct(order.shape, F32),
        in_specs=[vmem, vmem, vmem],
        out_specs=hbm,
        scratch_shapes=[
            pltpu.VMEM((SLOTS, ROWS, BLKS * LANES), F32),
            pltpu.SemaphoreType.DMA((SLOTS,)),
        ],
        compiler_params=pltpu.CompilerParams(vmem_limit_bytes=32 * 1024 * 1024),
        name="last",
    )(e1, u2, s2)


def solution(mesh):
    placed = (P("grain", "blk", None), P("grain"), P("grain"), P("blk", None))
    return jax.shard_map(
        body, mesh=mesh, in_specs=placed, out_specs=P("grain", "blk", None), check_vma=False
    )
```

profile of v0, /device:TPU:1, one launch (start us, length us, event | category | flops | bytes accessed | tf_op | source)
XLA Modules:
  0.0 36.4 jit_solution(363101277361057242)
XLA Ops:
  0.7 33.6 %steps.1 = (f32[18,16,32,128]{3,2,1,0:T(8,128)S(1)}, f32[16,16,32,128]{3,2,1,0:T(8,128)S(1)}, f32[16,32,128]{2,1,0:T(8,128)S(1)}) custom-call(f32[16,32,2048]{2,1,0:T(8,128)} %order.1, s32[16]{0:T(128)} %ids_hbm.1, s32[1]{0:T(128)S(6)} %copy.5.counts, s32[32,2048]{1,0:T(8,128)} %labels.1), custom_call_target="tpu_custom_call" | custom-call | tf_op jit(solution)/shard_map/steps/pallas_call | solution.py:437
  34.2 2.2 %last.1 = f32[16,32,2048]{2,1,0:T(8,128)} custom-call(f32[18,16,32,128]{3,2,1,0:T(8,128)S(1)} %get-tuple-element.8.e1, f32[16,16,32,128]{3,2,1,0:T(8,128)S(1)} %get-tuple-element.9.u2, f32[16,32,128]{2,1,0:T(8,128)S(1)} %get-tuple-element.10.s2), custom_call_target="tpu_custom_call" | custom-call | tf_op jit(solution)/shard_map/last/pallas_call | solution.py:484
where the time goes:
time: 36.5 us; the launch traced here: 36.4 us
  Pallas kernels  35.8 us (98%)
  between operations  0.66 us (2%)
    pallas_call x1, Pallas kernels, body(): pl.pallas_call(kernel, out_shape=(f32(SLOTS + 2, BLKS, ROWS, LANES), f32(...  33.6 us
    pallas_call x1, Pallas kernels, body(): pl.pallas_call(last, out_shape=jax.ShapeDtypeStruct(order.shape, F32), in...  2.2 us

commit v1 on v0

--- a/solution.py
+++ b/solution.py
@@ -89,15 +89,15 @@
         load(lax.rem(theirs + k, BLKS)).start()
         return carry
 
+    barrier = pltpu.get_barrier_semaphore()
+    for who in partners:
+        pl.semaphore_signal(barrier, inc=1, device_id=who, device_id_type=MESH)
+
     lax.fori_loop(0, BLKS, start_load, 0)
     ids_copy = pltpu.make_async_copy(ids_hbm, ids, small_sem)
     ids_copy.start()
     lab_copy = pltpu.make_async_copy(labels, lab, lab_sem)
     lab_copy.start()
-
-    barrier = pltpu.get_barrier_semaphore()
-    for who in partners:
-        pl.semaphore_signal(barrier, inc=1, device_id=who, device_id_type=MESH)
 
     stencil_weights(w)
     count = counts[0]
@@ -218,11 +218,11 @@
             s = s_lo + 2 * i
             planes(s + 1, yb)
             point(src, dst, dst_shift, s, ya)
-            planes(jnp.minimum(s + 2, s_hi - 1), ya)
+            planes(jnp.minimum(s + 2, SLOTS - 1), ya)
             point(src, dst, dst_shift, s + 1, yb)
             return carry
 
-        lax.fori_loop(0, (s_hi - s_lo) // 2, one, 0)
+        lax.fori_loop(0, lax.div(s_hi - s_lo, 2), one, 0)
 
     def sums_pass(j, carry):
         accp = [jnp.zeros((SUB, LANES), F32) for _ in range(TILES)]
@@ -276,22 +276,22 @@
                 u2f[where, :] = u2f[where, :] + 0.15 * out
         return carry
 
-    lax.fori_loop(0, HALF, first_pass, 0)
-    pl.semaphore_wait(barrier, len(partners))
-    core_s().start()
-    lax.fori_loop(HALF, BLKS, first_pass, 0)
-    for side in range(2):
-        halo("eta", h_eta, g_eta, side).start()
+    lax.fori_loop(0, BLKS, first_pass, 0)
     ids_copy.wait()
     lab_copy.wait()
     linear(e0f, e1f, 0, 0, 4)
+    pl.semaphore_wait(barrier, len(partners))
+    core_s().start()
+    for side in range(2):
+        halo("eta", h_eta, g_eta, side).start()
+    linear(e0f, e1f, 0, 4, 4 + 4)
 
     core_s().wait_recv()
     for d in (2, 1, 3):
         add_chunk(ps, r1s, d)
         x_s(d).start()
     add_chunk(ps, r1s, 0)
-    linear(e0f, e1f, 0, 4, SLOTS)
+    linear(e0f, e1f, 0, 4 + 4, SLOTS)
 
     lax.fori_loop(theirs, theirs + HALF, sums_pass, 0)
     core_pq().start()

time: 36.5 us -> 35.7 us (0.978)
  Pallas kernels: 35.8 us -> 34.9 us
    pallas_call x1, Pallas kernels: 33.6 us -> 32.7 us  [body(): pl.pallas_call(kernel, out_shape=(f32(SLOTS + 2, BLKS, ROWS, LANES), f32(...]
where the time goes in v1:
time: 35.7 us; the launch traced here: 35.6 us
  Pallas kernels  34.9 us (98%)
  between operations  0.66 us (2%)
    pallas_call x1, Pallas kernels, body(): pl.pallas_call(kernel, out_shape=(f32(SLOTS + 2, BLKS, ROWS, LANES), f32(...  32.7 us
    pallas_call x1, Pallas kernels, body(): pl.pallas_call(last, out_shape=jax.ShapeDtypeStruct(order.shape, F32), in...  2.2 us

profile of v1, /device:TPU:1, one launch (start us, length us, event | category | flops | bytes accessed | tf_op | source)
XLA Modules:
  0.0 35.6 jit_solution(11740292489784261397)
XLA Ops:
  0.7 32.7 %steps.1 = (f32[18,16,32,128]{3,2,1,0:T(8,128)S(1)}, f32[16,16,32,128]{3,2,1,0:T(8,128)S(1)}, f32[16,32,128]{2,1,0:T(8,128)S(1)}) custom-call(f32[16,32,2048]{2,1,0:T(8,128)} %order.1, s32[16]{0:T(128)} %ids_hbm.1, s32[1]{0:T(128)S(6)} %copy.5.counts, s32[32,2048]{1,0:T(8,128)} %labels.1), custom_call_target="tpu_custom_call" | custom-call | tf_op jit(solution)/shard_map/steps/pallas_call | solution.py:437
  33.4 2.2 %last.1 = f32[16,32,2048]{2,1,0:T(8,128)} custom-call(f32[18,16,32,128]{3,2,1,0:T(8,128)S(1)} %get-tuple-element.8.e1, f32[16,16,32,128]{3,2,1,0:T(8,128)S(1)} %get-tuple-element.9.u2, f32[16,32,128]{2,1,0:T(8,128)S(1)} %get-tuple-element.10.s2), custom_call_target="tpu_custom_call" | custom-call | tf_op jit(solution)/shard_map/last/pallas_call | solution.py:484

commit v2 on v1

--- a/solution.py
+++ b/solution.py
@@ -105,7 +105,7 @@
 
     e0f = e0.reshape((SLOTS + 2) * STRIDE, LANES)
     e1f = e1.reshape((SLOTS + 2) * STRIDE, LANES)
-    u2f = u2.reshape(SLOTS * STRIDE, LANES)
+    u2f = u2.reshape((SLOTS + 1) * STRIDE, LANES)
     sub = lax.broadcasted_iota(jnp.int32, (SUB, LANES), 0)
     lane = lax.broadcasted_iota(jnp.int32, (SUB, LANES), 1)
     low = lane < LANES // 2
@@ -279,19 +279,19 @@
     lax.fori_loop(0, BLKS, first_pass, 0)
     ids_copy.wait()
     lab_copy.wait()
-    linear(e0f, e1f, 0, 0, 4)
+    linear(e0f, e1f, 0, 0, 2)
     pl.semaphore_wait(barrier, len(partners))
     core_s().start()
     for side in range(2):
         halo("eta", h_eta, g_eta, side).start()
-    linear(e0f, e1f, 0, 4, 4 + 4)
+    linear(e0f, e1f, 0, 2, 6)
 
     core_s().wait_recv()
     for d in (2, 1, 3):
         add_chunk(ps, r1s, d)
         x_s(d).start()
     add_chunk(ps, r1s, 0)
-    linear(e0f, e1f, 0, 4 + 4, SLOTS)
+    linear(e0f, e1f, 0, 6, SLOTS)
 
     lax.fori_loop(theirs, theirs + HALF, sums_pass, 0)
     core_pq().start()
@@ -438,7 +438,7 @@
         kernel,
         out_shape=(
             f32(SLOTS + 2, BLKS, ROWS, LANES),
-            f32(SLOTS, BLKS, ROWS, LANES),
+            f32(SLOTS + 1, BLKS, ROWS, LANES),
             f32(BLKS, ROWS, LANES),
         ),
         in_specs=[hbm, hbm, smem, hbm],

time: 35.7 us -> 35.3 us (0.989)
    pallas_call x1, Pallas kernels: 32.7 us -> 32.4 us  [body(): pl.pallas_call(kernel, out_shape=(f32(SLOTS + 2, BLKS, ROWS, LANES), f32(...]
where the time goes in v2:
time: 35.3 us; the launch traced here: 35.2 us
  Pallas kernels  34.6 us (98%)
  between operations  0.66 us (2%)
    pallas_call x1, Pallas kernels, body(): pl.pallas_call(kernel, out_shape=(f32(SLOTS + 2, BLKS, ROWS, LANES), f32(...  32.4 us
    pallas_call x1, Pallas kernels, body(): pl.pallas_call(last, out_shape=jax.ShapeDtypeStruct(order.shape, F32), in...  2.2 us

profile of v2, /device:TPU:1, one launch (start us, length us, event | category | flops | bytes accessed | tf_op | source)
XLA Modules:
  0.0 35.2 jit_solution(1645401836639668894)
XLA Ops:
  0.7 32.4 %steps.1 = (f32[18,16,32,128]{3,2,1,0:T(8,128)S(1)}, f32[17,16,32,128]{3,2,1,0:T(8,128)S(1)}, f32[16,32,128]{2,1,0:T(8,128)S(1)}) custom-call(f32[16,32,2048]{2,1,0:T(8,128)} %order.1, s32[16]{0:T(128)} %ids_hbm.1, s32[1]{0:T(128)S(6)} %copy.5.counts, s32[32,2048]{1,0:T(8,128)} %labels.1), custom_call_target="tpu_custom_call" | custom-call | tf_op jit(solution)/shard_map/steps/pallas_call | solution.py:437
  33.0 2.2 %last.1 = f32[16,32,2048]{2,1,0:T(8,128)} custom-call(f32[18,16,32,128]{3,2,1,0:T(8,128)S(1)} %get-tuple-element.8.e1, f32[17,16,32,128]{3,2,1,0:T(8,128)S(1)} %get-tuple-element.9.u2, f32[16,32,128]{2,1,0:T(8,128)S(1)} %get-tuple-element.10.s2), custom_call_target="tpu_custom_call" | custom-call | tf_op jit(solution)/shard_map/last/pallas_call | solution.py:484
